TPU v7x, 32 devices: a whole 2x2x4 slice. The times are simulated.
32 devices in a mesh: dp: 16 (over z, y, core), group: 2 (over x).
Axes of the slice: x: 2, y: 2, z: 4, core: 2. Of those that a mesh axis runs over, the one named last changes fastest.
Arguments:
- tokens: bfloat16 [28224, 256], P('dp'), may hold values from -6 to 6
- cotangent: bfloat16 [28224, 256], P('dp'), may hold values from -6 to 6
- image_ids: int32 [16, 42, 42], P('dp'), may hold values from 0 to 63, as said below
- qkv_weight: float32 [2, 256, 768], P(None, None, 'group'), may hold values from -0.375 to 0.375
- proj_weight: float32 [2, 256, 256], P(None, 'group'), may hold values from -1 to 1
- up_weight: float32 [2, 256, 1024], P(None, None, 'group'), may hold values from -0.375 to 0.375
- down_weight: float32 [2, 1024, 256], P(None, 'group'), may hold values from -0.1875 to 0.1875
- shared_vectors: float32 [2, 1536], replicated
- group_vectors: float32 [2, 2, 2048], P(None, 'group'), may hold values from -3 to 3
- qkv_moment: float32 [2, 256, 768], P(None, 'dp', 'group'), may hold values from -320 to 320
- proj_moment: float32 [2, 256, 256], P(None, 'group', 'dp'), may hold values from -320 to 320
- up_moment: float32 [2, 256, 1024], P(None, 'dp', 'group'), may hold values from -320 to 320
- down_moment: float32 [2, 1024, 256], P(None, 'group', 'dp'), may hold values from -320 to 320
- shared_moment: float32 [2, 1536], P(None, 'dp'), may hold values from -512 to 512
- group_moment: float32 [2, 2, 2048], P(None, 'group', 'dp'), may hold values from -512 to 512
Outputs:
- outputs: bfloat16 [28224, 256], P('dp')
- input_grad: float32 [28224, 256], P('dp')
- qkv_momentum: float32 [2, 256, 768], P(None, 'dp', 'group')
- qkv_master: float32 [2, 256, 768], P(None, 'dp', 'group')
- proj_momentum: float32 [2, 256, 256], P(None, 'group', 'dp')
- proj_master: float32 [2, 256, 256], P(None, 'group', 'dp')
- up_momentum: float32 [2, 256, 1024], P(None, 'dp', 'group')
- up_master: float32 [2, 256, 1024], P(None, 'dp', 'group')
- down_momentum: float32 [2, 1024, 256], P(None, 'group', 'dp')
- down_master: float32 [2, 1024, 256], P(None, 'group', 'dp')
- shared_momentum: float32 [2, 1536], P(None, 'dp')
- shared_master: float32 [2, 1536], P(None, 'dp')
- group_momentum: float32 [2, 2, 2048], P(None, 'group', 'dp')
- group_master: float32 [2, 2, 2048], P(None, 'group', 'dp')
Inputs may be any that keep to these rules, and one draw needn't show every extreme that they name: `image_ids`: each canvas is cut into rectangles, one per image: its rows fall into bands and each band into pieces side by side. All tokens of one rectangle hold one number and different rectangles of a canvas hold different numbers; the bottom right rectangle of every canvas holds 63.
All inputs are finite; a program needn't handle non-finite values.
Results may differ from a plain program's by a relative error of at most 0.03.
Values may be sent and summed in bfloat16 or wider, within the bound.
No kernel may reach another device: no remote copies, remote signals or barrier semaphores. Data moves between devices by JAX's collectives and lax.ppermute only.
A program may use at most 192 MiB of HBM per device.

v0:
```python
import math

import jax
import jax.numpy as jnp
from jax import lax
from jax.sharding import PartitionSpec as P

HEADS = 8
STRIPE = 7
LAYERS = 2
NS_STEPS = 5
STRIPES_BLOCK = 2


epsilon = 1e-05
highest = lax.Precision.HIGHEST
coeff_first = 3.4445
coeff_second = -4.775
coeff_third = 2.0315
momentum_decay = 0.95
matrix_rate = 0.25
weight_decay = 0.1
vector_rate = 0.001
match_scale = 0.2
masked_score = -1e30


def from_root(block, axis, owner):
    block = jnp.where(lax.axis_index(axis) == owner, block, jnp.zeros_like(block))
    return lax.psum(block, axis)


def norm_rows(rows, gain, shift):
    mean = jnp.mean(rows, axis=-1, keepdims=True)
    centred = rows - mean
    spread = jnp.mean(centred * centred, axis=-1, keepdims=True)
    return centred * lax.rsqrt(spread + epsilon) * gain + shift


def gelu_exact(values):
    return jax.nn.gelu(values, approximate=False)


def position_term(values, ids, kernel, shift):
    side = values.shape[-2]
    padded = jnp.pad(values, ((0, 0), (1, 1), (1, 1), (0, 0)))
    padded_ids = jnp.pad(ids, ((0, 0), (1, 1), (1, 1)), constant_values=-1)
    band = jnp.arange(side) // STRIPE
    padded_band = jnp.pad(band, 1, constant_values=-1)
    total = jnp.zeros_like(values) + shift
    for tap in range(9):
        row_step = tap // 3
        col_step = tap % 3
        moved = padded[:, row_step : row_step + side, col_step : col_step + side]
        moved_ids = padded_ids[:, row_step : row_step + side, col_step : col_step + side]
        same_band = padded_band[row_step : row_step + side] == band
        valid = (moved_ids == ids) & same_band[None, :, None]
        total = total + jnp.where(valid[..., None], moved * kernel[tap], 0.0)
    return total


def contract_rows(left, right):
    return lax.dot_general(
        left, right, (((0,), (0,)), ((), ())), preferred_element_type=jnp.float32
    )


def contract_cols(left, right):
    return lax.dot_general(
        left, right, (((1,), (1,)), ((), ())), preferred_element_type=jnp.float32
    )


def newton(matrix):
    tall = matrix.shape[0] > matrix.shape[1]
    work = matrix.T if tall else matrix
    work = work / (jnp.sqrt(jnp.sum(work * work)) + 1e-07)
    for step in range(NS_STEPS):
        gram = jnp.dot(work, work.T, precision=highest)
        blend = coeff_second * gram + coeff_third * jnp.dot(gram, gram, precision=highest)
        work = coeff_first * work + jnp.dot(blend, work, precision=highest)
    return work.T if tall else work


def local(
    tokens,
    cotangent,
    image_ids,
    qkv_weight,
    proj_weight,
    up_weight,
    down_weight,
    shared_vectors,
    group_vectors,
    qkv_moment,
    proj_moment,
    up_moment,
    down_moment,
    shared_moment,
    group_moment,
):
    flip = lax.axis_index("group") == 1
    width = tokens.shape[1]
    channels = qkv_weight.shape[2] // 3
    heads_local = HEADS // 2
    head_size = channels // heads_local
    scale = head_size ** (-0.5)
    canvases = image_ids.shape[0]
    side = image_ids.shape[1]
    rows_total = tokens.shape[0]

    def to_frame(grid):
        return jnp.where(flip, jnp.swapaxes(grid, 1, 2), grid)

    def to_blocks(grid):
        return grid.reshape(-1, STRIPES_BLOCK, STRIPE * side, heads_local, head_size)

    def from_blocks(blocks):
        return blocks.reshape(canvases, side, side, channels)

    ids_frame = to_frame(image_ids)
    id_blocks = ids_frame.reshape(-1, STRIPES_BLOCK, STRIPE * side)

    def scores_of(query, keys_part, ids):
        scores = (
            jnp.einsum("sqhe,skhe->shqk", query, keys_part, preferred_element_type=jnp.float32)
            * scale
        )
        same = ids[:, None, :, None] == ids[:, None, None, :]
        return jnp.where(same, scores, masked_score)

    def attend(block):
        query, keys_part, values_part, ids = block
        scores = scores_of(query, keys_part, ids)
        top = jnp.max(scores, axis=-1, keepdims=True)
        expo = jnp.exp(scores - top)
        total = jnp.sum(expo, axis=-1, keepdims=True)
        weights = (expo / total).astype(jnp.bfloat16)
        mixed = jnp.einsum(
            "shqk,skhe->sqhe", weights, values_part, preferred_element_type=jnp.float32
        )
        return (mixed, top[..., 0] + jnp.log(total[..., 0]))

    def attend_back(block):
        query, keys_part, values_part, ids, logsum, grad_out = block
        weights = jnp.exp(scores_of(query, keys_part, ids) - logsum[..., None])
        grad_weights = jnp.einsum(
            "sqhe,skhe->shqk", grad_out, values_part, preferred_element_type=jnp.float32
        )
        grad_values = jnp.einsum(
            "shqk,sqhe->skhe",
            weights.astype(jnp.bfloat16),
            grad_out,
            preferred_element_type=jnp.float32,
        )
        grad_scores = weights * (
            grad_weights - jnp.sum(weights * grad_weights, axis=-1, keepdims=True)
        )
        grad_scores = grad_scores.astype(jnp.bfloat16)
        grad_query = (
            jnp.einsum(
                "shqk,skhe->sqhe", grad_scores, keys_part, preferred_element_type=jnp.float32
            )
            * scale
        )
        grad_keys = (
            jnp.einsum("shqk,sqhe->skhe", grad_scores, query, preferred_element_type=jnp.float32)
            * scale
        )
        return (grad_query, grad_keys, grad_values)

    def unpack_shared(layer):
        shared = shared_vectors[layer]
        return [shared[index * width : (index + 1) * width] for index in range(6)]

    def unpack_group(layer):
        vector = group_vectors[layer, 0]
        bias_query = vector[0:channels]
        bias_value = vector[channels : 2 * channels]
        position_shift = vector[2 * channels : 3 * channels]
        position_kernel = vector[3 * channels : 12 * channels].reshape(9, channels)
        up_bias = vector[12 * channels :]
        return (bias_query, bias_value, position_shift, position_kernel, up_bias)

    def backward(layer, grad_out, kept):
        (
            stream,
            inputs,
            query,
            keys_frame,
            values,
            logsum,
            heads,
            middle,
            inputs_second,
            hidden,
            active,
        ) = kept
        gain_first, shift_first, proj_bias, gain_second, shift_second, down_bias = unpack_shared(
            layer
        )
        bias_query, bias_value, position_shift, position_kernel, up_bias = unpack_group(layer)
        grad_mlp = grad_out.astype(jnp.bfloat16)
        grad_down_bias = jnp.sum(grad_mlp, axis=0, dtype=jnp.float32)
        grad_down = contract_rows(active, grad_mlp)
        grad_active = contract_cols(grad_mlp, down_weight[layer].astype(jnp.bfloat16))
        gelu_pull = jax.vjp(gelu_exact, hidden)[1]
        grad_hidden = gelu_pull(grad_active)[0].astype(jnp.bfloat16)
        grad_up_bias = jnp.sum(grad_hidden, axis=0, dtype=jnp.float32)
        grad_up = contract_rows(inputs_second, grad_hidden)
        partial_second = contract_cols(grad_hidden, up_weight[layer].astype(jnp.bfloat16))
        grad_inputs_second = lax.psum(partial_second.astype(jnp.bfloat16), "group").astype(
            jnp.float32
        )
        norm_pull = jax.vjp(norm_rows, middle, gain_second, shift_second)[1]
        grad_middle_norm, grad_gain_second, grad_shift_second = norm_pull(grad_inputs_second)
        grad_middle = grad_out + grad_middle_norm
        grad_branch = grad_middle.astype(jnp.bfloat16)
        grad_proj_bias = jnp.sum(grad_branch, axis=0, dtype=jnp.float32)
        grad_proj = contract_rows(heads, grad_branch)
        grad_heads = contract_cols(grad_branch, proj_weight[layer].astype(jnp.bfloat16)).astype(
            jnp.bfloat16
        )
        grad_frame = to_frame(grad_heads.reshape(canvases, side, side, channels))

        def position_local(values_wide, kernel, shift):
            return position_term(values_wide, ids_frame, kernel, shift)

        position_pull = jax.vjp(
            position_local, values.astype(jnp.float32), position_kernel, position_shift
        )[1]
        grad_values_position, grad_kernel, grad_position_shift = position_pull(
            grad_frame.astype(jnp.float32)
        )
        grad_query, grad_keys, grad_values = lax.map(
            attend_back,
            (
                to_blocks(query),
                to_blocks(keys_frame),
                to_blocks(values),
                id_blocks,
                logsum,
                to_blocks(grad_frame),
            ),
        )

        def unframe(grid):
            return to_frame(grid).reshape(rows_total, channels).astype(jnp.bfloat16)

        grad_query = unframe(from_blocks(grad_query))
        grad_keys = unframe(from_blocks(grad_keys))
        grad_values = unframe(from_blocks(grad_values) + grad_values_position)
        grad_mixed = jnp.concatenate([grad_query, grad_keys, grad_values], axis=1)
        grad_bias_query = jnp.sum(grad_query, axis=0, dtype=jnp.float32)
        grad_bias_value = jnp.sum(grad_values, axis=0, dtype=jnp.float32)
        grad_qkv = contract_rows(inputs, grad_mixed)
        partial_first = contract_cols(grad_mixed, qkv_weight[layer].astype(jnp.bfloat16))
        grad_inputs = lax.psum(partial_first.astype(jnp.bfloat16), "group").astype(jnp.float32)
        norm_pull_first = jax.vjp(norm_rows, stream, gain_first, shift_first)[1]
        grad_stream_norm, grad_gain_first, grad_shift_first = norm_pull_first(grad_inputs)
        grad_in = grad_middle + grad_stream_norm
        shared_grad = jnp.concatenate(
            [
                grad_gain_first,
                grad_shift_first,
                grad_proj_bias,
                grad_gain_second,
                grad_shift_second,
                grad_down_bias,
            ]
        )
        group_grad = jnp.concatenate(
            [
                grad_bias_query,
                grad_bias_value,
                grad_position_shift,
                grad_kernel.reshape(-1),
                grad_up_bias,
            ]
        )[None, :]
        return (grad_in, (grad_qkv, grad_proj, grad_up, grad_down, shared_grad, group_grad))

    stream = tokens.astype(jnp.float32)
    kept_all = []
    for layer in range(LAYERS):
        (
            forward_gain_first,
            forward_shift_first,
            forward_proj_bias,
            forward_gain_second,
            forward_shift_second,
            forward_down_bias,
        ) = unpack_shared(layer)
        (
            forward_bias_query,
            forward_bias_value,
            forward_position_shift,
            forward_position_kernel,
            forward_up_bias,
        ) = unpack_group(layer)
        forward_inputs = norm_rows(stream, forward_gain_first, forward_shift_first).astype(
            jnp.bfloat16
        )
        forward_mixed = jnp.dot(
            forward_inputs,
            qkv_weight[layer].astype(jnp.bfloat16),
            preferred_element_type=jnp.float32,
        )

        def framed(part):
            return to_frame(part.astype(jnp.bfloat16).reshape(canvases, side, side, channels))

        forward_query = framed(forward_mixed[:, :channels] + forward_bias_query)
        forward_keys_frame = framed(forward_mixed[:, channels : 2 * channels])
        forward_values = framed(forward_mixed[:, 2 * channels :] + forward_bias_value)
        attended, forward_logsum = lax.map(
            attend,
            (
                to_blocks(forward_query),
                to_blocks(forward_keys_frame),
                to_blocks(forward_values),
                id_blocks,
            ),
        )
        forward_total = from_blocks(attended) + position_term(
            forward_values.astype(jnp.float32),
            ids_frame,
            forward_position_kernel,
            forward_position_shift,
        )
        forward_heads = to_frame(forward_total).reshape(rows_total, channels).astype(jnp.bfloat16)
        part = jnp.dot(
            forward_heads,
            proj_weight[layer].astype(jnp.bfloat16),
            preferred_element_type=jnp.float32,
        )
        attention = lax.psum(part.astype(jnp.bfloat16), "group").astype(jnp.float32)
        forward_middle = stream + attention + forward_proj_bias
        forward_inputs_second = norm_rows(
            forward_middle, forward_gain_second, forward_shift_second
        ).astype(jnp.bfloat16)
        forward_hidden = (
            jnp.dot(
                forward_inputs_second,
                up_weight[layer].astype(jnp.bfloat16),
                preferred_element_type=jnp.float32,
            )
            + forward_up_bias
        )
        forward_active = gelu_exact(forward_hidden).astype(jnp.bfloat16)
        part_second = jnp.dot(
            forward_active,
            down_weight[layer].astype(jnp.bfloat16),
            preferred_element_type=jnp.float32,
        )
        forward_result = (
            forward_middle
            + lax.psum(part_second.astype(jnp.bfloat16), "group").astype(jnp.float32)
            + forward_down_bias
        )
        forward_kept = (
            stream,
            forward_inputs,
            forward_query,
            forward_keys_frame,
            forward_values,
            forward_logsum,
            forward_heads,
            forward_middle,
            forward_inputs_second,
            forward_hidden,
            forward_active,
        )
        stream = forward_result
        kept = forward_kept
        kept_all.append(kept)
    outputs = stream.astype(jnp.bfloat16)
    grad = cotangent.astype(jnp.float32)
    pieces = [None] * LAYERS
    for layer in reversed(range(LAYERS)):
        grad, grads = backward(layer, grad, kept_all[layer])
        pieces[layer] = grads
    stacked = [jnp.stack([pieces[layer][index] for layer in range(LAYERS)]) for index in range(6)]
    reduced = (
        lax.psum_scatter(stacked[0], "dp", scatter_dimension=1, tiled=True),
        lax.psum_scatter(stacked[1], "dp", scatter_dimension=2, tiled=True),
        lax.psum_scatter(stacked[2], "dp", scatter_dimension=1, tiled=True),
        lax.psum_scatter(stacked[3], "dp", scatter_dimension=2, tiled=True),
        lax.psum_scatter(stacked[4], "dp", scatter_dimension=1, tiled=True),
        lax.psum_scatter(stacked[5], "dp", scatter_dimension=2, tiled=True),
    )
    grad_qkv, grad_proj, grad_up, grad_down, grad_shared, grad_group = reduced
    moment_qkv = momentum_decay * qkv_moment + grad_qkv
    moment_proj = momentum_decay * proj_moment + grad_proj
    moment_up = momentum_decay * up_moment + grad_up
    moment_down = momentum_decay * down_moment + grad_down
    nesterov_qkv = grad_qkv + momentum_decay * moment_qkv
    nesterov_proj = grad_proj + momentum_decay * moment_proj
    nesterov_up = grad_up + momentum_decay * moment_up
    nesterov_down = grad_down + momentum_decay * moment_down
    whole = (
        lax.all_gather(nesterov_qkv, "dp", axis=1, tiled=True),
        lax.all_gather(nesterov_proj, "dp", axis=2, tiled=True),
        lax.all_gather(nesterov_up, "dp", axis=1, tiled=True),
        lax.all_gather(nesterov_down, "dp", axis=2, tiled=True),
    )
    index = lax.axis_index("dp")
    devices = lax.axis_size("dp")
    weights = (qkv_weight, proj_weight, up_weight, down_weight)
    matrix_dims = (0, 1, 0, 1)
    masters = []
    for which in range(4):
        layers_new = []
        for layer in range(LAYERS):
            matrix = whole[which][layer]
            owner = (layer * 4 + which) * devices // (4 * LAYERS)
            result = lax.cond(index == owner, newton, jnp.zeros_like, matrix)
            result = from_root(result.astype(jnp.bfloat16), "dp", owner).astype(result.dtype)
            axis_dim = matrix_dims[which]
            length = matrix.shape[axis_dim] // devices
            own = lax.dynamic_slice_in_dim(result, index * length, length, axis_dim)
            old = lax.dynamic_slice_in_dim(weights[which][layer], index * length, length, axis_dim)
            step_size = matrix_rate * match_scale * math.sqrt(max(matrix.shape))
            layers_new.append(old * (1.0 - matrix_rate * weight_decay) - step_size * own)
        masters.append(jnp.stack(layers_new))
    moment_shared = momentum_decay * shared_moment + grad_shared
    length_shared = shared_moment.shape[1]
    old_shared = lax.dynamic_slice_in_dim(shared_vectors, index * length_shared, length_shared, 1)
    master_shared = old_shared - vector_rate * moment_shared
    moment_group = momentum_decay * group_moment + grad_group
    length_group = group_moment.shape[2]
    old_group = lax.dynamic_slice_in_dim(group_vectors, index * length_group, length_group, 2)
    master_group = old_group - vector_rate * moment_group
    return (
        outputs,
        grad,
        moment_qkv,
        masters[0],
        moment_proj,
        masters[1],
        moment_up,
        masters[2],
        moment_down,
        masters[3],
        moment_shared,
        master_shared,
        moment_group,
        master_group,
    )


def solution(mesh):
    return jax.shard_map(
        local,
        mesh=mesh,
        in_specs=(
            P("dp", None),
            P("dp", None),
            P("dp", None, None),
            P(None, None, "group"),
            P(None, "group", None),
            P(None, None, "group"),
            P(None, "group", None),
            P(),
            P(None, "group", None),
            P(None, "dp", "group"),
            P(None, "group", "dp"),
            P(None, "dp", "group"),
            P(None, "group", "dp"),
            P(None, "dp"),
            P(None, "group", "dp"),
        ),
        out_specs=(
            P("dp", None),
            P("dp", None),
            P(None, "dp", "group"),
            P(None, "dp", "group"),
            P(None, "group", "dp"),
            P(None, "group", "dp"),
            P(None, "dp", "group"),
            P(None, "dp", "group"),
            P(None, "group", "dp"),
            P(None, "group", "dp"),
            P(None, "dp"),
            P(None, "dp"),
            P(None, "group", "dp"),
            P(None, "group", "dp"),
        ),
        check_vma=False,
    )
```

profile of v0, /device:TPU:0, one launch (start us, length us, event | category | flops | bytes accessed | tf_op | source)
XLA Modules:
  0.0 1223.2 jit_solution(8970654909900484519)
XLA Ops:
  37.5 14.7 %while.52 = (s32[]{:T(128)}, f32[3,2,294,4,32]{2,4,3,1,0:T(8,128)}, f32[3,2,4,294]{3,2,1,0:T(4,128)S(1)}, bf16[3,2,294,4,32]{2,4,3,1,0:T(8,128)(2,1)}, s32[3,2,2...) while((s32[]{:T(128)}, f32[3,2,294,4,32]{2,4,3,1,0:T(8,128)}, ...), condition=%wide.region_5.6_spmd, body=%wide.region_2.5_spmd.sunk | while | flops 96978840 | bytes 10119941 | solution.py:316
  71.9 37.1 %all-reduce.55.cloned.1.call-done = bf16[1764,256]{1,0:T(8,128)(2,1)} async-done(((bf16[1764,256]{1,0:T(8,128)(2,1)}), bf16[1764,256]{1,0:T(8,128)(2,1)}) %all-reduce.55.cloned.1.call-update) | async-done | bytes 903184 | tf_op jit(solution)/shard_map/psum | solution.py:337
  111.5 10.5 multiply_convert_fusion.3
  125.0 37.2 %all-reduce.57.cloned.1.call-done = bf16[1764,256]{1,0:T(8,128)(2,1)} async-done(((bf16[1764,256]{1,0:T(8,128)(2,1)}), bf16[1764,256]{1,0:T(8,128)(2,1)}) %all-reduce.57.cloned.1.call-update) | async-done | bytes 903184 | tf_op jit(solution)/shard_map/psum | solution.py:358
  196.0 14.8 %while.53 = (s32[]{:T(128)}, f32[3,2,294,4,32]{2,4,3,1,0:T(8,128)}, f32[3,2,4,294]{3,2,1,0:T(4,128)S(1)}, bf16[3,2,294,4,32]{2,4,3,1,0:T(8,128)(2,1)}, s32[3,2,2...) while((s32[]{:T(128)}, f32[3,2,294,4,32]{2,4,3,1,0:T(8,128)}, ...), condition=%wide.region_15.16_spmd, body=%wide.region_12.15_spmd.sunk | while | flops 96978840 | bytes 10119941 | solution.py:316
  219.4 10.6 add_add_fusion.9
  237.5 34.9 %all-reduce.59.cloned.1.call-done = bf16[1764,256]{1,0:T(8,128)(2,1)} async-done(((bf16[1764,256]{1,0:T(8,128)(2,1)}), bf16[1764,256]{1,0:T(8,128)(2,1)}) %all-reduce.59.cloned.1.call-update) | async-done | bytes 903184 | tf_op jit(solution)/shard_map/psum | solution.py:337
  295.1 33.0 %all-reduce.61.cloned.1.call-done = bf16[1764,256]{1,0:T(8,128)(2,1)} async-done(((bf16[1764,256]{1,0:T(8,128)(2,1)}), bf16[1764,256]{1,0:T(8,128)(2,1)}) %all-reduce.61.cloned.1.call-update) | async-done | bytes 903184 | tf_op jit(solution)/shard_map/psum | solution.py:212
  338.8 13.8 %fusion.279 = (f32[128]{0:T(128)S(1)}, f32[128]{0:T(128)S(1)}, f32[128]{0:T(128)S(1)}, f32[128]{0:T(128)S(1)}, f32[128]{0:T(128)S(1)}, /*index=5*/f32[128]{0:T(1...) fusion(f32[1,42,42,128]{3,2,1,0:T(8,128)} %get-tuple-element.62, ...), kind=kLoop, calls=%fused_computation.522 | loop fusion | flops 6772480 | bytes 2728737 | tf_op jit(solution)/shard_map/transpose(jvp())/reduce_sum | solution.py:58
  363.1 25.8 %while.54 = (s32[]{:T(128)}, bf16[3,2,294,4,32]{2,1,0,4,3:T(2,128)(2,1)}, bf16[3,2,294,4,32]{2,1,0,4,3:T(2,128)(2,1)}, f32[3,2,294,4,32]{2,4,3,1,0:T(8,128)}, bf...) while((s32[]{:T(128)}, ...), condition=%wide.region_25.26_spmd, body=%wide.region_23.25_spmd.sunk | while | flops 227971136 | bytes 25712916 | solution.py:235
  449.3 33.6 %all-reduce.63.cloned.1.call-done = bf16[1764,256]{1,0:T(8,128)(2,1)} async-done(((bf16[1764,256]{1,0:T(8,128)(2,1)}), bf16[1764,256]{1,0:T(8,128)(2,1)}) %all-reduce.63.cloned.1.call-update) | async-done | bytes 903184 | tf_op jit(solution)/shard_map/psum | solution.py:258
  508.3 26.9 %all-reduce.65.cloned.1.call-done = bf16[1764,256]{1,0:T(8,128)(2,1)} async-done(((bf16[1764,256]{1,0:T(8,128)(2,1)}), bf16[1764,256]{1,0:T(8,128)(2,1)}) %all-reduce.65.cloned.1.call-update) | async-done | bytes 903184 | tf_op jit(solution)/shard_map/psum | solution.py:212
  572.5 28.2 %while.55 = (s32[]{:T(128)}, bf16[3,2,294,4,32]{2,1,0,4,3:T(2,128)(2,1)}, bf16[3,2,294,4,32]{2,1,0,4,3:T(2,128)(2,1)}, f32[3,2,294,4,32]{2,4,3,1,0:T(8,128)}, bf...) while((s32[]{:T(128)}, ...), condition=%wide.region_34.35_spmd, body=%wide.region_32.34_spmd.sunk | while | flops 227971136 | bytes 27519280 | solution.py:235
  669.8 57.8 %all-reduce.67.cloned.1.call-done = (f32[2,128,256]{1,0,2:T(2,128)}, f32[2,512,256]{1,0,2:T(2,128)}) async-done(((f32[2,128,256]{1,0,2:T(2,128)}, f32[2,512,256]{1,0,2:T(2,128)}), (f32[2,128,256]{1,0,2:T(2,128)}, f32[2,512,256]{1,0,2:T(2,128)})) %all-reduce.67.cloned.1.call-update) | async-done | bytes 1310736
  729.5 59.2 %reduce-scatter.15.cloned.1.call-done = f32[128,2]{1,0:T(8,128)} async-done(((f32[2048,2]{1,0:T(8,128)}), f32[128,2]{1,0:T(8,128)}) %reduce-scatter.15.cloned.1.call-update) | async-done | bytes 1040
  791.8 20.1 %all_gather.15 = f32[2,128,256]{1,0,2:T(2,128)S(1)} all-gather(f32[2,128,16]{1,0,2:T(2,128)S(1)} %get-tuple-element.611), channel_id=1, replica_groups=mesh['dp'=16,'group'=2] {'dp'}, dimensions={2}, use_global_device_ids=true | all-gather | bytes 278528 | tf_op jit(solution)/shard_map/all_gather | solution.py:403
  814.7 34.5 %reduce-scatter.11.cloned.1.call-done = f32[2,16,512]{2,1,0:T(8,128)} async-done(((f32[2,256,512]{2,1,0:T(8,128)}), f32[2,16,512]{2,1,0:T(8,128)}) %reduce-scatter.11.cloned.1.call-update) | async-done | bytes 65552 | tf_op jit(solution)/shard_map/reduce_scatter | solution.py:387
  850.7 57.4 %reduce-scatter.9.cloned.1.call-done = f32[2,16,384]{2,1,0:T(8,128)} async-done(((f32[2,256,384]{2,1,0:T(8,128)}), f32[2,16,384]{2,1,0:T(8,128)}) %reduce-scatter.9.cloned.1.call-update) | async-done | bytes 49168 | tf_op jit(solution)/shard_map/reduce_scatter | solution.py:385
  909.5 21.7 %all_gather.13 = f32[2,256,384]{2,1,0:T(8,128)S(1)} all-gather(f32[2,16,384]{2,1,0:T(8,128)S(1)} %get-tuple-element.613), channel_id=1, replica_groups=mesh['dp'=16,'group'=2] {'dp'}, dimensions={1}, use_global_device_ids=true | all-gather | bytes 835584 | tf_op jit(solution)/shard_map/all_gather | solution.py:402
  942.6 24.5 %all-reduce.71.cloned.1.call-done = (bf16[1764,256]{1,0:T(8,128)(2,1)}, bf16[1764,256]{1,0:T(8,128)(2,1)}) async-done(((bf16[1764,256]{1,0:T(8,128)(2,1)}, bf16[1764,256]{1,0:T(8,128)(2,1)}), (bf16[1764,256]{1,0:T(8,128)(2,1)}, bf16[1764,256]{1,0:T(8,128)(2,1)})) %all-reduce.71.cloned.1.call-update) | async-done | bytes 1806352 | tf_op jit(solution)/shard_map/psum | solution.py:358
  972.9 34.6 %all-gather.5.cloned.1.call-done = f32[2,512,256]{1,0,2:T(2,128)} async-done(((f32[2,512,16]{1,0,2:T(2,128)}), f32[2,512,256]{1,0,2:T(2,128)}) %all-gather.5.cloned.1.call-update) | async-done | bytes 1048592 | tf_op jit(solution)/shard_map/all_gather | solution.py:405
  1016.1 30.7 %all-gather.3.cloned.1.call-done = f32[2,256,512]{2,1,0:T(8,128)} async-done(((f32[2,16,512]{2,1,0:T(8,128)}), f32[2,256,512]{2,1,0:T(8,128)}) %all-gather.3.cloned.1.call-update) | async-done | bytes 1048592 | tf_op jit(solution)/shard_map/all_gather | solution.py:404
  1063.0 43.1 %reduce-scatter.13.cloned.1.call-done = f32[96,2]{1,0:T(8,128)} async-done(((f32[1536,2]{1,0:T(8,128)}), f32[96,2]{1,0:T(8,128)}) %reduce-scatter.13.cloned.1.call-update) | async-done | bytes 784
  1108.3 99.4 %all-reduce.69.cloned.1.call-done = (bf16[256,384]{1,0:T(8,128)(2,1)}, bf16[256,384]{1,0:T(8,128)(2,1)}, bf16[128,256]{0,1:T(8,128)(2,1)}, bf16[128,256]{0,1:T(8...) async-done(((bf16[256,384]{1,0:T(8,128)(2,1)}, bf16[256,384]{1,0:T(8,128)(2,1)}, ...) | async-done | bytes 1572880 | tf_op jit(solution)/shard_map/psum | solution.py:30
  (785 shorter events, 493.3 us)
Async XLA Ops:
  7.2 101.8 %all-reduce.55.cloned.1.call-start = ((), (), s32[]{:S(2)}) async-start(), calls=%async_computation.4 | async-start | bytes 1810432 | tf_op jit(solution)/shard_map/psum | solution.py:337
  11.1 100.4 %copy-start.107 = (f32[1,256]{1,0:T(1,128)}, f32[1,256]{1,0:T(1,128)S(1)}, u32[]{:S(2)}) copy-start(f32[1,256]{1,0:T(1,128)S(1)} %get-tuple-element.723) | copy-start | bytes 3076
  11.1 100.4 %copy-start.182 = (f32[1,256]{1,0:T(1,128)}, f32[1,256]{1,0:T(1,128)S(1)}, u32[]{:S(2)}) copy-start(f32[1,256]{1,0:T(1,128)S(1)} %get-tuple-element.722) | copy-start | bytes 3076
  11.1 151.1 %copy-start.100 = (f32[1,256]{1,0:T(1,128)}, f32[1,256]{1,0:T(1,128)S(1)}, u32[]{:S(2)}) copy-start(f32[1,256]{1,0:T(1,128)S(1)} %get-tuple-element.724) | copy-start | bytes 3076
  11.1 476.5 %copy-start.109 = (f32[1,256]{1,0:T(1,128)}, f32[1,256]{1,0:T(1,128)S(1)}, u32[]{:S(2)}) copy-start(f32[1,256]{1,0:T(1,128)S(1)} %get-tuple-element.720) | copy-start | bytes 3076
  69.2 92.9 %all-reduce.57.cloned.1.call-start = ((), (), s32[]{:S(2)}) async-start(), calls=%async_computation.5 | async-start | bytes 1810432 | tf_op jit(solution)/shard_map/psum | solution.py:358
  124.8 147.6 %all-reduce.59.cloned.1.call-start = ((), (), s32[]{:S(2)}) async-start(), calls=%async_computation.6 | async-start | bytes 1810432 | tf_op jit(solution)/shard_map/psum | solution.py:337
  125.0 209.7 %copy-start.71 = (f32[1,128,256]{1,2,0:T(8,128)}, f32[1,128,256]{1,2,0:T(8,128)S(1)}, u32[]{:S(2)}) copy-start(f32[1,128,256]{1,2,0:T(8,128)S(1)} %copy.448) | copy-start | bytes 393220
  235.2 92.9 %all-reduce.61.cloned.1.call-start = ((), (), s32[]{:S(2)}) async-start(), calls=%async_computation.7 | async-start | bytes 1810432 | tf_op jit(solution)/shard_map/psum | solution.py:212
  290.8 192.1 %all-reduce.63.cloned.1.call-start = ((), (), s32[]{:S(2)}) async-start(), calls=%async_computation.8 | async-start | bytes 1810432 | tf_op jit(solution)/shard_map/psum | solution.py:258
  445.6 89.6 %all-reduce.65.cloned.1.call-start = ((), (), s32[]{:S(2)}) async-start(), calls=%async_computation.9 | async-start | bytes 1810432 | tf_op jit(solution)/shard_map/psum | solution.py:212
  497.9 229.8 %all-reduce.67.cloned.1.call-start = ((), (), s32[]{:S(2)}) async-start(), calls=%async_computation.16 | async-start | bytes 2621440
  633.6 155.1 %reduce-scatter.15.cloned.1.call-start = ((), (), s32[]{:S(2)}) async-start(), calls=%async_computation.15 | async-start | bytes 1114112
  641.9 207.3 %reduce-scatter.11.cloned.1.call-start = ((), (), s32[]{:S(2)}) async-start(), calls=%async_computation.11 | async-start | bytes 1114112 | tf_op jit(solution)/shard_map/reduce_scatter | solution.py:387
  644.1 264.0 %reduce-scatter.9.cloned.1.call-start = ((), (), s32[]{:S(2)}) async-start(), calls=%async_computation.10 | async-start | bytes 835584 | tf_op jit(solution)/shard_map/reduce_scatter | solution.py:385
  661.7 305.5 %all-reduce.71.cloned.1.call-start = ((), (), s32[]{:S(2)}) async-start(), calls=%async_computation.18 | async-start | bytes 3620864 | tf_op jit(solution)/shard_map/psum | solution.py:358
  666.6 340.9 %all-gather.5.cloned.1.call-start = ((), (), s32[]{:S(2)}) async-start(), calls=%async_computation.13 | async-start | bytes 1114112 | tf_op jit(solution)/shard_map/all_gather | solution.py:405
  668.0 61.4 %copy-start.158 = (f32[256]{0:T(256)S(1)}, f32[256]{0:T(256)}, u32[]{:S(2)}) copy-start(f32[256]{0:T(256)} %get-tuple-element.655) | copy-start | bytes 3076
  668.0 121.8 %copy-start.184 = (f32[2,1,128]{2,1,0:T(1,128)S(1)}, f32[2,1,128]{2,1,0:T(1,128)}, u32[]{:S(2)}) copy-start(f32[2,1,128]{2,1,0:T(1,128)} %param.53) | copy-start | bytes 3076
  668.0 123.0 %copy-start.111 = (f32[2,128,16]{1,2,0:T(8,128)S(1)}, f32[2,128,16]{1,2,0:T(8,128)}, u32[]{:S(2)}) copy-start(f32[2,128,16]{1,2,0:T(8,128)} %param.49) | copy-start | bytes 49156
  729.3 317.6 %all-gather.3.cloned.1.call-start = ((), (), s32[]{:S(2)}) async-start(), calls=%async_computation.12 | async-start | bytes 1114112 | tf_op jit(solution)/shard_map/all_gather | solution.py:404
  813.3 94.8 %copy-start.103 = (f32[2,16,384]{2,1,0:T(8,128)S(1)}, f32[2,16,384]{2,1,0:T(8,128)}, u32[]{:S(2)}) copy-start(f32[2,16,384]{2,1,0:T(8,128)} %param.48) | copy-start | bytes 147460
  850.7 255.4 %reduce-scatter.13.cloned.1.call-start = ((), (), s32[]{:S(2)}) async-start(), calls=%async_computation.14 | async-start | bytes 835584
  972.9 234.8 %all-reduce.69.cloned.1.call-start = ((), (), s32[]{:S(2)}) async-start(), calls=%async_computation.17 | async-start | bytes 3145728 | tf_op jit(solution)/shard_map/psum | solution.py:30
  (179 other events, 1852.6 us)
Sparse Core Ops, SparseCore 0:
  69.3 39.5 all-reduce.54
  124.9 37.1 all-reduce.56
  235.3 37.0 all-reduce.58
  290.9 37.1 all-reduce.60
  445.7 37.1 all-reduce.62
  498.0 37.1 all-reduce.64
  633.7 93.9 all-reduce.66
  731.3 57.3 reduce-scatter.14
  792.7 56.3 reduce-scatter.10
  852.6 55.4 reduce-scatter.8
  911.3 55.8 all-reduce.70
  969.4 38.1 all-gather.4
  1010.0 36.8 all-gather.2
  1050.7 55.3 reduce-scatter.12
  1111.5 96.1 all-reduce.68
where the time goes:
time: 1240 us; the launch traced here: 1220 us
  waiting for transfers between devices  644 us (52%)
  local copies, waits for them, and re-layouts  207 us (17%)
  other arithmetic  157 us (13%)
  matrix products  141 us (11%)
  blocking collectives  41.8 us (3%)
  between operations  17.7 us (1%)
  loops' own time  13.5 us (1%)
    unnamed x18, waiting for transfers between devices  160 us
    psum x1, waiting for transfers between devices, from_root(): return lax.psum(block, axis)  99.4 us
    psum x2, waiting for transfers between devices, local(): attention = lax.psum(part.astype(jnp.bfloat16), 'group').astype(jnp.float32)  71.9 us
    reshape x20, local copies, waits for them, and re-layouts, from_blocks(): return blocks.reshape(canvases, side, side, channels)  69.5 us
    psum x2, waiting for transfers between devices, local(): lax.psum(part_second.astype(jnp.bfloat16), 'group').astype(jnp.float32)  61.7 us
    psum x2, waiting for transfers between devices, backward(): lax.psum(partial_second.astype(jnp.bfloat16), 'group').astype(jnp.float32)  60 us
    reduce_scatter x1, waiting for transfers between devices, local(): lax.psum_scatter(stacked[0], 'dp', scatter_dimension=1, tiled=True)  57.4 us
    unnamed x412, local copies, waits for them, and re-layouts  36.8 us
  transfers between devices with their start and end apart: 15, of which 15 were waited for; matrix products, arithmetic and copies ran while one was open for 8% of the time, Pallas kernels for 0%

commit v1 on v0

v1 whole, which is shorter than its diff:
```python
import functools
import math

import jax
import jax.numpy as jnp
from jax import lax
from jax.experimental import pallas as pl
from jax.experimental.pallas import tpu as pltpu
from jax.sharding import PartitionSpec as P

HEADS = 8
STRIPE = 7
LAYERS = 2
NS_STEPS = 5

epsilon = 1e-05
coeff_first = 3.4445
coeff_second = -4.775
coeff_third = 2.0315
momentum_decay = 0.95
matrix_rate = 0.25
weight_decay = 0.1
vector_rate = 0.001
match_scale = 0.2
masked_score = -1e30

f32 = jnp.float32
bf16 = jnp.bfloat16
LOG2E = 1.4426950408889634
VMEM_LIMIT = 62 * 1024 * 1024

SIDE = 42
NS = 6
SLOT = 8
ROWS = SIDE * SLOT
KEYS = 384
WIDTH = 256
CH = 128
HALF = 512
HL = 4
HEAD = 32


def dot(a, b):
    return jnp.dot(a, b, preferred_element_type=f32)


def dot_t(a, b):
    return lax.dot_general(a, b, (((1,), (1,)), ((), ())), preferred_element_type=f32)


def dot_rows(a, b):
    return lax.dot_general(a, b, (((0,), (0,)), ((), ())), preferred_element_type=f32)


def lane_head():
    return lax.broadcasted_iota(jnp.int32, (1, CH), 1) // HEAD


def stripe_of(ref, g, s):
    if g == 0:
        block = ref[pl.ds(STRIPE * s, STRIPE)]
    else:
        block = ref[:, pl.ds(s, 1)]
    return block.reshape(ROWS, block.shape[-1])


def put_stripe(ref, g, s, value):
    if g == 0:
        ref[pl.ds(STRIPE * s, STRIPE)] = value.reshape(STRIPE, NS, SLOT, value.shape[-1])
    else:
        ref[:, pl.ds(s, 1)] = value.reshape(SIDE, 1, SLOT, value.shape[-1])


def normed(rows):
    mean = jnp.mean(rows, axis=-1, keepdims=True)
    centred = rows - mean
    spread = jnp.mean(centred * centred, axis=-1, keepdims=True)
    rstd = lax.rsqrt(spread + epsilon)
    return centred * rstd, rstd


def norm_back(grad, hat, rstd, gain):
    scaled = grad * gain
    first = jnp.mean(scaled, axis=-1, keepdims=True)
    second = jnp.mean(scaled * hat, axis=-1, keepdims=True)
    return rstd * (scaled - first - hat * second)


def tile_sum(rows):
    return jnp.sum(rows.reshape(-1, SLOT, rows.shape[-1]), axis=0)


def gelu_parts(x):
    z = jnp.abs(x)
    bell = jnp.exp2(x * x * (-0.5 * LOG2E))
    t = 1.0 / (1.0 + (0.3275911 * math.sqrt(0.5)) * z)
    poly = 0.5 * 1.061405429
    for coeff in (-1.453152027, 1.421413741, -0.284496736, 0.254829592):
        poly = poly * t + 0.5 * coeff
    tail = poly * t * bell
    phi = jnp.where(x >= 0.0, 1.0 - tail, tail)
    return x * phi, phi + x * bell * (1.0 / math.sqrt(2.0 * math.pi))


def fine_shifts(x, g):
    axis = x.ndim - 2
    one_up = pltpu.roll(x, SLOT - 1, axis)
    one_down = pltpu.roll(x, 1, axis)
    if g == 1:
        return one_up, one_down
    place = lax.broadcasted_iota(jnp.int32, (1, 1, SLOT, 1), 2)
    after = jnp.concatenate([x[:, 1:], x[:, :1]], axis=1)
    before = jnp.concatenate([x[:, -1:], x[:, :-1]], axis=1)
    up = jnp.where(place == STRIPE - 1, pltpu.roll(after, STRIPE - 1, axis), one_up)
    down = jnp.where(place == 0, pltpu.roll(before, 2, axis), one_down)
    return up, down


def coarse(x, step):
    if step == 0:
        return x
    zero = jnp.zeros_like(x[:1])
    if step > 0:
        return jnp.concatenate([x[1:], zero], axis=0)
    return jnp.concatenate([zero, x[:-1]], axis=0)


def masked_neighbours(x, ids, g):
    shape = (STRIPE, NS, SLOT, CH) if g == 0 else (SIDE, SLOT, CH)
    x = x.reshape(shape)
    up, down = fine_shifts(x, g)
    centre = ids[0].reshape(shape)
    around = {0: (x, centre), 1: (up, ids[1].reshape(shape)), -1: (down, ids[2].reshape(shape))}
    for row_step in (-1, 0, 1):
        for col_step in (-1, 0, 1):
            tap = 3 * (row_step + 1) + col_step + 1
            coarse_step, fine_step = (row_step, col_step) if g == 0 else (col_step, row_step)
            source, source_ids = around[fine_step]
            if coarse_step == 0 and fine_step == 0:
                yield tap, source.reshape(ROWS, CH)
                continue
            if coarse_step != 0:
                source = coarse(source, coarse_step)
                zero = jnp.full_like(source_ids[:1], -9.0)
                parts = [source_ids[1:], zero] if coarse_step > 0 else [zero, source_ids[:-1]]
                source_ids = jnp.concatenate(parts, axis=0)
            kept = jnp.where(source_ids == centre, source, 0.0)
            yield tap, kept.reshape(ROWS, CH)


def block_diagonal(x):
    head = lane_head()
    zero = jnp.zeros((KEYS - ROWS, CH), f32)
    parts = []
    for h in range(HL):
        parts += [jnp.where(head == h, x, 0.0), zero]
    return jnp.concatenate(parts, axis=0).astype(bf16)


def take_diagonal(x):
    head = lane_head()
    total = jnp.where(head == 0, x[0:ROWS], 0.0)
    for h in range(1, HL):
        total = jnp.where(head == h, x[h * KEYS : h * KEYS + ROWS], total)
    return total


def ids_of(idb, g, s):
    names = (0, 1, 2) if g == 0 else (0, 3, 4)
    return [stripe_of(idb.at[n], g, s) for n in names]


def fill_weights(own, wq, wqo, wp, wpo, gv, gvo, wq2, wp2, gv2, layer):
    other = 1 - own
    wq2[own] = wq[0]
    wq2[other] = wqo[0]
    wp2[own] = wp[0]
    wp2[other] = wpo[0]
    gv2[own] = gv[layer]
    gv2[other] = gvo[layer]


def forward_kernel(
    layer, own_ref, stream, wq, wqo, wp, wpo, wu, wuo, wd, wdo, sv, gv, gvo, idb, idrow,
    out, mid, qkv_s, e_s, rl_s, att_s, heads_s, active_s, dgelu_s, wq2, wp2, gv2,
):
    own = own_ref[0]
    fill_weights(own, wq, wqo, wp, wpo, gv, gvo, wq2, wp2, gv2, layer)

    def shared(index):
        return sv[layer : layer + 1, index * WIDTH : (index + 1) * WIDTH]

    for g in range(2):
        def stripe(s, carry, g=g):
            i = g * NS + s
            rows = stripe_of(stream, g, s)
            hat, _ = normed(rows)
            a1 = (hat * shared(0) + shared(1)).astype(bf16)
            mixed = dot(a1, wq2[g])
            vec = gv2[g]
            q = ((mixed[:, :CH] + vec[:, :CH]) * (HEAD ** -0.5 * LOG2E)).astype(bf16)
            k = mixed[:, CH : 2 * CH].astype(bf16)
            v = (mixed[:, 2 * CH :] + vec[:, CH : 2 * CH]).astype(bf16)
            qkv_s[i, :, 0:CH] = q
            qkv_s[i, :, CH : 2 * CH] = k
            qkv_s[i, :, 2 * CH :] = v
            ids = ids_of(idb, g, s)
            key_ids = idrow[i]
            bias = jnp.where(jnp.concatenate([ids[0]] * 3, axis=1) == key_ids, 0.0, masked_score)
            scores = dot_t(q, block_diagonal(k.astype(f32)))
            parts = []
            for h in range(HL):
                score = scores[:, h * KEYS : (h + 1) * KEYS] + bias
                top = jnp.max(score, axis=-1, keepdims=True)
                parts.append(jnp.exp2(score - top).astype(bf16))
            e = jnp.concatenate(parts, axis=1)
            e_s[i] = e
            vf = v.astype(f32)
            ones = block_diagonal(jnp.ones((ROWS, CH), f32))
            both = dot(e, jnp.concatenate([block_diagonal(vf), ones], axis=1))
            rl = 1.0 / both[:, CH:]
            att = both[:, :CH] * rl
            rl_s[i] = rl
            att_s[i] = att.astype(bf16)
            total = att + vec[:, 2 * CH : 3 * CH]
            for tap, near in masked_neighbours(vf, ids, g):
                total = total + near * vec[:, (3 + tap) * CH : (4 + tap) * CH]
            heads = total.astype(bf16)
            heads_s[i] = heads
            part = dot(heads, wp2[g]).astype(bf16).astype(f32)
            if g == 0:
                put_stripe(mid, g, s, part)
            else:
                put_stripe(mid, g, s, rows + (stripe_of(mid, g, s) + part + shared(2)))
            return carry

        lax.fori_loop(0, NS, stripe, 0)

    def block(s, carry):
        rows = stripe_of(mid, 0, s)
        hat, _ = normed(rows)
        a2 = (hat * shared(3) + shared(4)).astype(bf16)
        parts = []
        for slot, (up, down, vec) in enumerate(((wu, wd, gv), (wuo, wdo, gvo))):
            hidden = dot(a2, up[0]) + vec[layer][:, 12 * CH :]
            active, slope = gelu_parts(hidden)
            active = active.astype(bf16)
            if slot == 0:
                active_s[s] = active
            dgelu_s[slot, s] = slope.astype(bf16)
            parts.append(dot(active, down[0]).astype(bf16).astype(f32))
        put_stripe(out, 0, s, rows + ((parts[0] + parts[1]) + shared(5)))
        return carry

    lax.fori_loop(0, NS, block, 0)


def backward_kernel(
    layer, own_ref, grad, stream, mid, qkv_s, e_s, rl_s, att_s, heads_s, active_s, dgelu_s,
    wq, wqo, wp, wpo, wu, wuo, wd, wdo, sv, gv, gvo, idb,
    grad_in, big, svec, gvec,
    wq2, wp2, gv2, gmid, gb, da1, a1_own, dqkv_own, gb_own, a2_s, gh_s, gm_s, acc_s, acc_b1, acc_g,
):
    own = own_ref[0]
    fill_weights(own, wq, wqo, wp, wpo, gv, gvo, wq2, wp2, gv2, layer)
    acc_s[...] = jnp.zeros_like(acc_s)
    acc_b1[...] = jnp.zeros_like(acc_b1)
    acc_g[...] = jnp.zeros_like(acc_g)

    def shared(index):
        return sv[layer : layer + 1, index * WIDTH : (index + 1) * WIDTH]

    def block(s, carry):
        rows = stripe_of(grad, 0, s)
        gm = rows.astype(bf16)
        gm_s[s] = gm
        acc_s[5] += tile_sum(gm.astype(f32))
        hat, rstd = normed(stripe_of(mid, 0, s))
        a2_s[s] = (hat * shared(3) + shared(4)).astype(bf16)
        parts = []
        for slot, (up, down) in enumerate(((wu, wd), (wuo, wdo))):
            gh = (dot_t(gm, down[0]) * dgelu_s[slot, s].astype(f32)).astype(bf16)
            if slot == 0:
                gh_s[s] = gh
                acc_b1[...] += tile_sum(gh.astype(f32))
            parts.append(dot_t(gh, up[0]).astype(bf16).astype(f32))
        da2 = parts[0] + parts[1]
        acc_s[3] += tile_sum(da2 * hat)
        acc_s[4] += tile_sum(da2)
        new = rows + norm_back(da2, hat, rstd, shared(3))
        put_stripe(gmid, 0, s, new)
        low = new.astype(bf16).astype(f32)
        put_stripe(gb, 0, s, low)
        acc_s[2] += tile_sum(low)
        return carry

    lax.fori_loop(0, NS, block, 0)

    lanes = lax.broadcasted_iota(jnp.int32, (CH, CH), 1)
    rows_of = lax.broadcasted_iota(jnp.int32, (CH, CH), 0)
    gather = jnp.where((lanes % HEAD == rows_of // HEAD) & (lanes < 3 * HEAD), 1.0, 0.0).astype(bf16)
    gather = jnp.concatenate([gather, gather], axis=0)

    for g in range(2):
        def stripe(s, carry, g=g):
            i = g * NS + s
            hat, _ = normed(stripe_of(stream, g, s))
            a1 = (hat * shared(0) + shared(1)).astype(bf16)
            gbs = stripe_of(gb, g, s).astype(bf16)
            vec = gv2[g]
            d_out = dot_t(gbs, wp2[g]).astype(bf16).astype(f32)
            q = qkv_s[i, :, 0:CH]
            k = qkv_s[i, :, CH : 2 * CH]
            v = qkv_s[i, :, 2 * CH :]
            vf = v.astype(f32)
            scaled = (d_out * rl_s[i]).astype(bf16)
            prod = scaled.astype(f32) * att_s[i].astype(f32)
            prod_high = prod.astype(bf16)
            prod_low = (prod - prod_high.astype(f32)).astype(bf16)
            centre = dot(jnp.concatenate([prod_high, prod_low], axis=1), gather)
            first = centre.astype(bf16).astype(f32)
            rest = centre - first
            second = rest.astype(bf16).astype(f32)
            lane = lax.broadcasted_iota(jnp.int32, (1, CH), 1)
            pieces = jnp.where(lane < HEAD, first, jnp.where(lane < 2 * HEAD, second, rest - second))
            left = jnp.concatenate([scaled, (-pieces).astype(bf16)], axis=1)
            marks = []
            for h in range(HL):
                mark = jnp.where((lane % HEAD == h) & (lane < 3 * HEAD), 1.0, 0.0)
                marks.append(jnp.broadcast_to(mark, (KEYS, CH)))
            marks = jnp.concatenate(marks, axis=0).astype(bf16)
            right = jnp.concatenate([block_diagonal(vf), marks], axis=1)
            e = e_s[i]
            ds = (e.astype(f32) * dot_t(left, right)).astype(bf16)
            dq = (dot(ds, block_diagonal(k.astype(f32))) * HEAD ** -0.5).astype(bf16)
            dk = (take_diagonal(dot_rows(ds, q)) * (1.0 / LOG2E)).astype(bf16)
            dv = take_diagonal(dot_rows(e, scaled))
            ids = ids_of(idb, g, s)
            for tap, near in masked_neighbours(d_out, ids, g):
                mirror = 8 - tap
                dv = dv + near * vec[:, (3 + mirror) * CH : (4 + mirror) * CH]
                acc_g[g, 3 + mirror] += tile_sum(near * vf)
            dv = dv.astype(bf16)
            acc_g[g, 0] += tile_sum(dq.astype(f32))
            acc_g[g, 1] += tile_sum(dv.astype(f32))
            acc_g[g, 2] += tile_sum(d_out)
            dqkv = jnp.concatenate([dq, dk, dv], axis=1)
            part = dot_t(dqkv, wq2[g]).astype(bf16).astype(f32)
            if g == 0:
                put_stripe(da1, g, s, part)
            else:
                put_stripe(da1, g, s, stripe_of(da1, g, s) + part)

            @pl.when(own == g)
            def _():
                a1_own[s] = a1
                dqkv_own[s] = dqkv
                gb_own[s] = gbs

            return carry

        lax.fori_loop(0, NS, stripe, 0)

    def last(s, carry):
        hat, rstd = normed(stripe_of(stream, 0, s))
        da = stripe_of(da1, 0, s)
        acc_s[0] += tile_sum(da * hat)
        acc_s[1] += tile_sum(da)
        put_stripe(grad_in, 0, s, stripe_of(gmid, 0, s) + norm_back(da, hat, rstd, shared(0)))
        return carry

    lax.fori_loop(0, NS, last, 0)

    def flat(ref):
        return ref[...].reshape(NS * ROWS, ref.shape[-1])

    heads = heads_s[pl.ds(own * NS, NS)].reshape(NS * ROWS, CH)
    big[:, 0:384] = dot_rows(flat(a1_own), flat(dqkv_own)).astype(bf16)
    big[:, 384:512] = dot_rows(flat(gb_own), heads).astype(bf16)
    big[:, 512:1024] = dot_rows(flat(a2_s), flat(gh_s)).astype(bf16)
    big[:, 1024:1536] = dot_rows(flat(gm_s), flat(active_s)).astype(bf16)
    for index in range(6):
        svec[:, index * WIDTH : (index + 1) * WIDTH] = jnp.sum(acc_s[index], axis=0, keepdims=True)
    for index in range(12):
        gvec[:, index * CH : (index + 1) * CH] = jnp.sum(acc_g[own, index], axis=0, keepdims=True)
    gvec[:, 12 * CH :] = jnp.sum(acc_b1[...], axis=0, keepdims=True)


def sds(shape, dtype):
    return jax.ShapeDtypeStruct(shape, dtype)


CANVAS = (SIDE, NS, SLOT, WIDTH)
SAVED = [
    sds(CANVAS, f32),
    sds((2 * NS, ROWS, 3 * CH), bf16),
    sds((2 * NS, ROWS, HL * KEYS), bf16),
    sds((2 * NS, ROWS, CH), f32),
    sds((2 * NS, ROWS, CH), bf16),
    sds((2 * NS, ROWS, CH), bf16),
    sds((NS, ROWS, HALF), bf16),
    sds((2, NS, ROWS, HALF), bf16),
]
PAIR_SCRATCH = [
    pltpu.VMEM((2, WIDTH, 3 * CH), bf16),
    pltpu.VMEM((2, CH, WIDTH), bf16),
    pltpu.VMEM((2, 1, 16 * CH), f32),
]


def specs(n):
    return [pl.BlockSpec(memory_space=pltpu.SMEM)] + [pl.BlockSpec(memory_space=pltpu.VMEM)] * n


def run_forward(layer, own, args):
    return pl.pallas_call(
        functools.partial(forward_kernel, layer),
        out_shape=[sds(CANVAS, f32)] + SAVED,
        in_specs=specs(len(args)),
        out_specs=[pl.BlockSpec(memory_space=pltpu.VMEM)] * (1 + len(SAVED)),
        scratch_shapes=PAIR_SCRATCH,
        compiler_params=pltpu.CompilerParams(vmem_limit_bytes=VMEM_LIMIT),
        cost_estimate=pl.CostEstimate(flops=8 * 10**9, bytes_accessed=40 * 10**6, transcendentals=0),
        name=f"layer{layer}_forward",
    )(own, *args)


def run_backward(layer, own, args):
    return pl.pallas_call(
        functools.partial(backward_kernel, layer),
        out_shape=[
            sds(CANVAS, f32),
            sds((WIDTH, 12 * CH), bf16),
            sds((1, 6 * WIDTH), f32),
            sds((1, 16 * CH), f32),
        ],
        in_specs=specs(len(args)),
        out_specs=[pl.BlockSpec(memory_space=pltpu.VMEM)] * 4,
        scratch_shapes=PAIR_SCRATCH
        + [
            pltpu.VMEM(CANVAS, f32),
            pltpu.VMEM(CANVAS, f32),
            pltpu.VMEM(CANVAS, f32),
            pltpu.VMEM((NS, ROWS, WIDTH), bf16),
            pltpu.VMEM((NS, ROWS, 3 * CH), bf16),
            pltpu.VMEM((NS, ROWS, WIDTH), bf16),
            pltpu.VMEM((NS, ROWS, WIDTH), bf16),
            pltpu.VMEM((NS, ROWS, HALF), bf16),
            pltpu.VMEM((NS, ROWS, WIDTH), bf16),
            pltpu.VMEM((6, SLOT, WIDTH), f32),
            pltpu.VMEM((SLOT, HALF), f32),
            pltpu.VMEM((2, 12, SLOT, CH), f32),
        ],
        compiler_params=pltpu.CompilerParams(vmem_limit_bytes=VMEM_LIMIT),
        cost_estimate=pl.CostEstimate(flops=16 * 10**9, bytes_accessed=40 * 10**6, transcendentals=0),
        name=f"layer{layer}_backward",
    )(own, *args)


def split_dot(a, b, dims):
    a_high, b_high = a.astype(bf16), b.astype(bf16)
    a_low = (a - a_high.astype(f32)).astype(bf16)
    b_low = (b - b_high.astype(f32)).astype(bf16)

    def one(x, y):
        return lax.dot_general(x, y, (dims, ((), ())), preferred_element_type=f32)

    return one(a_high, b_high) + (one(a_high, b_low) + one(a_low, b_high))


def newton_kernel(spans, big, out):
    works = []
    for (start, stop), turned in spans:
        work = big[:, start:stop].astype(f32)
        if turned:
            work = work.T
        works.append(work / (jnp.sqrt(jnp.sum(work * work)) + 1e-07))
    for _ in range(NS_STEPS):
        grams = [split_dot(work, work, ((1,), (1,))) for work in works]
        blends = [
            coeff_second * gram + coeff_third * split_dot(gram, gram, ((1,), (0,))) for gram in grams
        ]
        works = [
            coeff_first * work + split_dot(blend, work, ((1,), (0,)))
            for work, blend in zip(works, blends)
        ]
    for ((start, stop), turned), work in zip(spans, works):
        out[:, start:stop] = work.T if turned else work


def run_newton(big, spans):
    return pl.pallas_call(
        functools.partial(newton_kernel, spans),
        out_shape=sds(big.shape, f32),
        in_specs=[pl.BlockSpec(memory_space=pltpu.VMEM)],
        out_specs=pl.BlockSpec(memory_space=pltpu.VMEM),
        compiler_params=pltpu.CompilerParams(vmem_limit_bytes=VMEM_LIMIT),
        cost_estimate=pl.CostEstimate(flops=7 * 10**9, bytes_accessed=3 * 10**6, transcendentals=0),
        name="newton",
    )(big)


def swap(x, axis, bit):
    n = lax.axis_size(axis)
    return lax.ppermute(x, axis, [(i, i ^ bit) for i in range(n)])


def scatter_sum(chunks):
    n = chunks.shape[0]
    me = lax.axis_index("dp")
    bit = 1
    while bit < n:
        halves = chunks.reshape((chunks.shape[0] // 2, 2) + chunks.shape[1:])
        side = (me // bit) % 2
        send = lax.dynamic_index_in_dim(halves, 1 - side, 1, False)
        keep = lax.dynamic_index_in_dim(halves, side, 1, False)
        got = swap(send, "dp", bit)
        bit *= 2
        total = keep.astype(f32) + got.astype(f32)
        chunks = total.astype(bf16) if bit < n else total
    return chunks[0]


def gather_rows(mine):
    n = lax.axis_size("dp")
    me = lax.axis_index("dp")
    held = mine[None]
    bit = n // 2
    while bit >= 1:
        side = (me // bit) % 2
        got = swap(held, "dp", bit)
        first = jnp.where(side == 0, held, got)
        second = jnp.where(side == 0, got, held)
        held = jnp.stack([first, second], axis=1).reshape((-1,) + mine.shape)
        bit //= 2
    return held.reshape((-1,) + mine.shape[1:])


def padded(rows):
    grid = rows.astype(f32).reshape(SIDE, NS, STRIPE, WIDTH)
    return jnp.pad(grid, ((0, 0), (0, 0), (0, 1), (0, 0)))


def unpadded(grid):
    return grid[:, :, :STRIPE].reshape(SIDE * SIDE, WIDTH)


def local(
    tokens, cotangent, image_ids, qkv_weight, proj_weight, up_weight, down_weight, shared_vectors, group_vectors,
    qkv_moment, proj_moment, up_moment, down_moment, shared_moment, group_moment,
):
    own = lax.axis_index("group").astype(jnp.int32).reshape(1)
    devices = lax.axis_size("dp")
    index = lax.axis_index("dp")

    masters = (qkv_weight, proj_weight, up_weight, down_weight)
    weights = []
    for layer in range(LAYERS):
        pairs = []
        for master in masters:
            mine = master[layer : layer + 1].astype(bf16)
            pairs += [mine, swap(mine, "group", 1)]
        weights.append(pairs)
    other_vectors = swap(group_vectors, "group", 1)

    ids = image_ids[0].astype(f32)
    edge = jnp.full((SIDE, 1), -3.0, f32)
    right = jnp.concatenate([ids[:, 1:], edge], axis=1)
    left = jnp.concatenate([edge, ids[:, :-1]], axis=1)
    column = jnp.arange(SIDE) % STRIPE
    inner_right = jnp.where(column == STRIPE - 1, -3.0, right)
    inner_left = jnp.where(column == 0, -3.0, left)

    def cells(grid, fill):
        grid = grid.reshape(SIDE, NS, STRIPE)
        return jnp.pad(grid, ((0, 0), (0, 0), (0, 1)), constant_values=fill)

    centre = cells(ids, -1.0)
    grids = jnp.stack([centre] + [cells(grid, -3.0) for grid in (right, left, inner_right, inner_left)])
    idb = jnp.broadcast_to(grids[..., None], grids.shape + (CH,))
    rows_h = centre.reshape(NS, ROWS)
    rows_v = jnp.swapaxes(centre, 0, 1).reshape(NS, ROWS)
    idrow = jnp.concatenate([rows_h, rows_v], axis=0)
    idrow = jnp.pad(idrow, ((0, 0), (0, KEYS - ROWS)), constant_values=-5.0)[:, None, :]

    vectors = (shared_vectors, group_vectors, other_vectors)
    stream = padded(tokens)
    grad = padded(cotangent)
    streams, saved = [stream], []
    for layer in range(LAYERS):
        result = run_forward(layer, own, (streams[-1], *weights[layer], *vectors, idb, idrow))
        streams.append(result[0])
        saved.append(result[1:])
    outputs = unpadded(streams[-1]).astype(bf16)
    bigs, svecs, gvecs = [None] * LAYERS, [None] * LAYERS, [None] * LAYERS
    for layer in reversed(range(LAYERS)):
        grad, bigs[layer], svecs[layer], gvecs[layer] = run_backward(
            layer, own, (grad, streams[layer], *saved[layer], *weights[layer], *vectors, idb)
        )
    input_grad = unpadded(grad)

    rows_each = WIDTH // devices
    length_shared = shared_moment.shape[1]
    length_group = group_moment.shape[2]
    out = [[] for _ in range(12)]
    for layer in range(LAYERS):
        pack = jnp.concatenate(
            [svecs[layer].reshape(devices, length_shared), gvecs[layer].reshape(devices, length_group)], axis=1
        ).astype(bf16)
        width = 2 * CH
        pack = jnp.pad(pack, ((0, 0), (0, width - pack.shape[1])))[:, None, :]
        pack = jnp.pad(pack, ((0, 0), (0, rows_each - 1), (0, 0)))
        chunks = jnp.concatenate([bigs[layer].reshape(devices, rows_each, 12 * CH), pack], axis=2)
        total = scatter_sum(chunks)
        matrix = total[:, : 12 * CH]
        moment = jnp.concatenate(
            [qkv_moment[layer], proj_moment[layer].T, up_moment[layer], down_moment[layer].T], axis=1
        )
        moment_new = momentum_decay * moment + matrix
        whole = gather_rows((matrix + momentum_decay * moment_new).astype(bf16))
        ortho = run_newton(
            whole,
            (((0, 384), False), ((384, 512), True), ((512, 1024), False), ((1024, 1536), False)),
        )
        own_rows = lax.dynamic_slice_in_dim(ortho, index * rows_each, rows_each, 0)
        spans = ((0, 384, False), (384, 512, True), (512, 1024, False), (1024, 1536, True))
        for which, (start, stop, turned) in enumerate(spans):
            fresh = moment_new[:, start:stop]
            step = own_rows[:, start:stop]
            master = masters[which][layer]
            if turned:
                fresh, step = fresh.T, step.T
            old = lax.dynamic_slice_in_dim(master, index * rows_each, rows_each, 1 if turned else 0)
            size = matrix_rate * match_scale * math.sqrt(max(master.shape))
            out[2 * which].append(fresh)
            out[2 * which + 1].append(old * (1.0 - matrix_rate * weight_decay) - size * step)
        grad_shared = total[0, 12 * CH : 12 * CH + length_shared]
        grad_group = total[0, 12 * CH + length_shared : 12 * CH + length_shared + length_group][None]
        moment_shared = momentum_decay * shared_moment[layer] + grad_shared
        moment_group = momentum_decay * group_moment[layer] + grad_group
        old_shared = lax.dynamic_slice_in_dim(shared_vectors[layer], index * length_shared, length_shared, 0)
        old_group = lax.dynamic_slice_in_dim(group_vectors[layer], index * length_group, length_group, 1)
        out[8].append(moment_shared)
        out[9].append(old_shared - vector_rate * moment_shared)
        out[10].append(moment_group)
        out[11].append(old_group - vector_rate * moment_group)
    return (outputs, input_grad, *[jnp.stack(parts) for parts in out])


def solution(mesh):
    return jax.shard_map(
        local,
        mesh=mesh,
        in_specs=(
            P("dp", None),
            P("dp", None),
            P("dp", None, None),
            P(None, None, "group"),
            P(None, "group", None),
            P(None, None, "group"),
            P(None, "group", None),
            P(),
            P(None, "group", None),
            P(None, "dp", "group"),
            P(None, "group", "dp"),
            P(None, "dp", "group"),
            P(None, "group", "dp"),
            P(None, "dp"),
            P(None, "group", "dp"),
        ),
        out_specs=(
            P("dp", None),
            P("dp", None),
            P(None, "dp", "group"),
            P(None, "dp", "group"),
            P(None, "group", "dp"),
            P(None, "group", "dp"),
            P(None, "dp", "group"),
            P(None, "dp", "group"),
            P(None, "group", "dp"),
            P(None, "group", "dp"),
            P(None, "dp"),
            P(None, "dp"),
            P(None, "group", "dp"),
            P(None, "group", "dp"),
        ),
        check_vma=False,
    )
```

time: 1240 us -> 321 us (0.26)
  waiting for transfers between devices: 644 us -> 20.5 us
  Pallas kernels: 0 us -> 200 us
  local copies, waits for them, and re-layouts: 207 us -> 41.2 us
  matrix products: 141 us -> 0 us
  other arithmetic: 157 us -> 22 us
  blocking collectives: 41.8 us -> 0 us
  starting transfers between devices: 1.22 us -> 30.4 us
  between operations: 17.7 us -> 1.7 us
  loops' own time: 13.5 us -> 0 us
    psum x8 -> x0, waiting for transfers between devices: 327 us -> none  [the longest x1 99.4 us: from_root(): return lax.psum(block, axis)]
    pallas_call x0 -> x6, Pallas kernels: none -> 200 us  [the longest x2 97.2 us: run_backward(): pl.pallas_call(functools.partial(backward_kernel, layer), out_shape=[sds(...]
    unnamed x18 -> x0, waiting for transfers between devices: 160 us -> none
    dot_general x81 -> x0, matrix products: 141 us -> none  [the longest x8 21.6 us: contract_rows(): lax.dot_general(left, right, (((0,), (0,)), ((), ())), preferred_element_...]
    reshape x37 -> x11, local copies, waits for them, and re-layouts: 100 us -> 3.92 us  [the longest x1 2.91 us: unpadded(): return grid[:, :, :STRIPE].reshape(SIDE * SIDE, WIDTH)]
    reduce_scatter x2 -> x0, waiting for transfers between devices: 91.9 us -> none  [the longest x1 57.4 us: local(): lax.psum_scatter(stacked[0], 'dp', scatter_dimension=1, tiled=True)]
    reduce_sum x31 -> x0, other arithmetic: 66.2 us -> none  [the longest x2 21.5 us: position_term(): total = total + jnp.where(valid[..., None], moved * kernel[tap], 0.0)]
    all_gather x2 -> x0, waiting for transfers between devices: 65.4 us -> none  [the longest x1 34.6 us: local(): lax.all_gather(nesterov_down, 'dp', axis=2, tiled=True)]
  transfers between devices with their start and end apart: 15 -> 25, of which waited for: 15 -> 8; matrix products, arithmetic and copies ran while one was open for 8% -> 14% of each run, Pallas kernels for 0% -> 16%
where the time goes in v1:
time: 321 us; the launch traced here: 316 us
  Pallas kernels  200 us (62%)
  local copies, waits for them, and re-layouts  41.2 us (13%)
  starting transfers between devices  30.4 us (9%)
  other arithmetic  22 us (7%)
  waiting for transfers between devices  20.5 us (6%)
    pallas_call x2, Pallas kernels, run_backward(): pl.pallas_call(functools.partial(backward_kernel, layer), out_shape=[sds(...  97.2 us
    pallas_call x2, Pallas kernels, run_forward(): pl.pallas_call(functools.partial(forward_kernel, layer), out_shape=[sds(C...  79.9 us
    ppermute x25, starting transfers between devices, swap(): return lax.ppermute(x, axis, [(i, i ^ bit) for i in range(n)])  30.4 us
    pallas_call x2, Pallas kernels, run_newton(): pl.pallas_call(functools.partial(newton_kernel, spans), out_shape=sds(big...  23.4 us
    ppermute x25, waiting for transfers between devices, swap(): return lax.ppermute(x, axis, [(i, i ^ bit) for i in range(n)])  20.5 us
    another operation x21, other arithmetic, local(): return (outputs, input_grad, *[jnp.stack(parts) for parts in out])  14.1 us
    slice x6, local copies, waits for them, and re-layouts, local(): mine = master[layer:layer + 1].astype(bf16)  7.77 us
  transfers between devices with their start and end apart: 25, of which 8 were waited for; matrix products, arithmetic and copies ran while one was open for 14% of the time, Pallas kernels for 16%

profile of v1, /device:TPU:0, one launch (start us, length us, event | category | flops | bytes accessed | tf_op | source)
XLA Modules:
  0.0 316.3 jit_solution(1618028574192933279)
XLA Ops:
  0.7 2.0 fusion.66
  2.7 2.9 collective-permute-start
  8.9 2.1 collective-permute-start.2
  13.3 1.9 collective-permute-start.4
  31.6 1.8 copy.179.wd
  38.8 1.9 collective-permute-start.8
  43.3 1.9 collective-permute-start.7
  45.3 3.6 %broadcast_in_dim.37.idb = f32[5,42,6,8,128]{4,3,2,1,0:T(8,128)} broadcast(f32[5,42,6,8]{3,2,1,0:T(8,128)S(1)} %copy.174), dimensions={0,1,2,3} | broadcast | bytes 5201280 | tf_op jit(solution)/shard_map/broadcast_in_dim | solution.py:581
  48.9 40.1 %layer0_forward.1 = (f32[42,6,8,256]{3,2,1,0:T(8,128)}, f32[42,6,8,256]{3,2,1,0:T(8,128)}, bf16[12,336,384]{2,1,0:T(8,128)(2,1)}, bf16[12,336,1536]{2,1,0:T(8,12...) custom-call(s32[1]{0:T(128)} %bitcast.own_ref, ...), custom_call_target="tpu_custom_call" | custom-call | flops 8000000000 | bytes 40000000 | tf_op jit(solution)/shard_map/layer0_forward/pallas_call | solution.py:417
  89.9 39.8 %layer1_forward.1 = (f32[42,6,8,256]{3,2,1,0:T(8,128)}, f32[42,6,8,256]{3,2,1,0:T(8,128)}, bf16[12,336,384]{2,1,0:T(8,128)(2,1)}, bf16[12,336,1536]{2,1,0:T(8,12...) custom-call(s32[1]{0:T(128)} %bitcast.own_ref, ...), custom_call_target="tpu_custom_call" | custom-call | flops 8000000000 | bytes 40000000 | tf_op jit(solution)/shard_map/layer1_forward/pallas_call | solution.py:417
  132.6 48.8 %layer1_backward.1 = (f32[42,6,8,256]{3,2,1,0:T(8,128)}, bf16[256,1536]{1,0:T(8,128)(2,1)}, f32[1,1536]{1,0:T(1,128)}, f32[1,2048]{1,0:T(1,128)}) custom-call(s32[1]{0:T(128)} %bitcast.own_ref, f32[42,6,8,256]{3,2,1,0:T(8,128)} %pad_convert_fusion.grad, f32[42,6,8,256]{3,2,1,0:T(8,128)} %get-tuple-element.40.stream, ...), custom_call_target="tpu_custom_call" | custom-call | flops 16000000000 | bytes 40000000 | tf_op jit(solution)/shard_map/layer1_backward/pallas_call | solution.py:430
  181.4 48.4 %layer0_backward.1 = (f32[42,6,8,256]{3,2,1,0:T(8,128)}, bf16[256,1536]{1,0:T(8,128)(2,1)}, f32[1,1536]{1,0:T(1,128)}, f32[1,2048]{1,0:T(1,128)}) custom-call(s32[1]{0:T(128)} %bitcast.own_ref, f32[42,6,8,256]{3,2,1,0:T(8,128)} %get-tuple-element.50.grad, f32[42,6,8,256]{3,2,1,0:T(8,128)} %pad_convert_fusion.1.stream, ...), custom_call_target="tpu_custom_call" | custom-call | flops 16000000000 | bytes 40000000 | tf_op jit(solution)/shard_map/layer0_backward/pallas_call | solution.py:430
  229.8 2.9 reshape.214
  238.7 6.1 %collective-permute-done.14 = bf16[4,16,1792]{2,1,0:T(8,128)(2,1)S(1)} collective-permute-done((bf16[4,16,1792]{2,1,0:T(8,128)(2,1)S(1)}, bf16[4,16,1792]{2,1,0:T(8,128)(2,1)S(1)}, u32[]{:S(2)}, u32[]{:S(2)}) %collective-permute-start.14) | collective-permute-done | bytes 229408 | tf_op jit(solution)/shard_map/ppermute | solution.py:506
  246.6 2.4 collective-permute-done.10
  250.7 2.6 collective-permute-start.16
  254.5 2.2 collective-permute-start.12
  256.9 2.8 collective-permute-done.12
  259.8 2.3 collective-permute-start.21
  271.3 2.5 collective-permute-done.22
  277.0 2.6 collective-permute-done.23
  279.8 1.9 collective-permute-done.19
  283.0 11.6 %newton.3 = f32[256,1536]{1,0:T(8,128)} custom-call(bf16[256,1536]{1,0:T(8,128)(2,1)} %bitcast.310), custom_call_target="tpu_custom_call" | custom-call | flops 7000000000 | bytes 3000000 | tf_op jit(solution)/shard_map/newton/pallas_call | solution.py:493
  295.7 11.8 %newton.2 = f32[256,1536]{1,0:T(8,128)} custom-call(bf16[256,1536]{1,0:T(8,128)(2,1)} %bitcast.311), custom_call_target="tpu_custom_call" | custom-call | flops 7000000000 | bytes 3000000 | tf_op jit(solution)/shard_map/newton/pallas_call | solution.py:493
  (234 shorter events, 67.5 us)
Async XLA Ops:
  2.7 42.6 %collective-permute-start = (bf16[1,256,384]{2,1,0:T(8,128)(2,1)}, bf16[1,256,384]{2,1,0:T(8,128)(2,1)}, u32[]{:S(2)}, u32[]{:S(2)}) collective-permute-start(bf16[1,256,384]{2,1,0:T(8,128)(2,1)} %get-tuple-element.87.wq), channel_id=1, source_target_pairs={{0,1},{1,0},{2,3},{3,2},{4,5},{5,4},{6,7},{7,6},{8,9},{9,8},{10,11... | collective-permute-start | bytes 589832 | tf_op jit(solution)/shard_map/ppermute | solution.py:506
  8.0 21.9 %collective-permute-start.1 = (bf16[1,128,256]{1,2,0:T(8,128)(2,1)}, bf16[1,128,256]{1,2,0:T(8,128)(2,1)}, u32[]{:S(2)}, u32[]{:S(2)}) collective-permute-start(bf16[1,128,256]{1,2,0:T(8,128)(2,1)} %convert_element_type.146), channel_id=1, source_target_pairs={{0,1},{1,0},{2,3},{3,2},{4,5},{5,4},{6,7},{7,6},{8,9},{9,8},{10,11... | collective-permute-start | bytes 196616 | tf_op jit(solution)/shard_map/ppermute | solution.py:506
  8.9 36.4 %collective-permute-start.2 = (bf16[1,256,512]{2,1,0:T(8,128)(2,1)}, bf16[1,256,512]{2,1,0:T(8,128)(2,1)}, u32[]{:S(2)}, u32[]{:S(2)}) collective-permute-start(bf16[1,256,512]{2,1,0:T(8,128)(2,1)} %get-tuple-element.79.wu), channel_id=1, source_target_pairs={{0,1},{1,0},{2,3},{3,2},{4,5},{5,4},{6,7},{7,6},{8,9},{9,8},{10,11... | collective-permute-start | bytes 786440 | tf_op jit(solution)/shard_map/ppermute | solution.py:506
  13.2 28.3 %collective-permute-start.3 = (bf16[1,512,256]{1,2,0:T(8,128)(2,1)}, bf16[1,512,256]{1,2,0:T(8,128)(2,1)}, u32[]{:S(2)}, u32[]{:S(2)}) collective-permute-start(bf16[1,512,256]{1,2,0:T(8,128)(2,1)} %convert_element_type.148), channel_id=1, source_target_pairs={{0,1},{1,0},{2,3},{3,2},{4,5},{5,4},{6,7},{7,6},{8,9},{9,8},{10,11... | collective-permute-start | bytes 786440 | tf_op jit(solution)/shard_map/ppermute | solution.py:506
  13.3 30.1 %collective-permute-start.4 = (f32[2,1,2048]{2,1,0:T(1,128)}, f32[2,1,2048]{2,1,0:T(1,128)}, u32[]{:S(2)}, u32[]{:S(2)}) collective-permute-start(f32[2,1,2048]{2,1,0:T(1,128)} %gv.7), channel_id=1, source_target_pairs={{0,1},{1,0},{2,3},{3,2},{4,5},{5,4},{6,7},{7,6},{8,9},{9,8},{10,11... | collective-permute-start | bytes 49160 | tf_op jit(solution)/shard_map/ppermute | solution.py:506
  29.9 8.8 %collective-permute-start.6 = (bf16[1,128,256]{1,2,0:T(8,128)(2,1)S(1)}, bf16[1,128,256]{1,2,0:T(8,128)(2,1)S(1)}, u32[]{:S(2)}, u32[]{:S(2)}) collective-permute-start(bf16[1,128,256]{1,2,0:T(8,128)(2,1)S(1)} %convert_element_type.153), channel_id=1, source_target_pairs={{0,1},{1,0},{2,3},{3,2},{4,5},{5,4},{6,7},{7,6},{8,9},{9,8},{10,11... | collective-permute-start | bytes 196616 | tf_op jit(solution)/shard_map/ppermute | solution.py:506
  38.8 50.3 %collective-permute-start.8 = (bf16[1,512,256]{1,2,0:T(8,128)(2,1)S(1)}, bf16[1,512,256]{1,2,0:T(8,128)(2,1)S(1)}, u32[]{:S(2)}, u32[]{:S(2)}) collective-permute-start(bf16[1,512,256]{1,2,0:T(8,128)(2,1)S(1)} %convert_element_type.155), channel_id=1, source_target_pairs={{0,1},{1,0},{2,3},{3,2},{4,5},{5,4},{6,7},{7,6},{8,9},{9,8},{10,11... | collective-permute-start | bytes 786440 | tf_op jit(solution)/shard_map/ppermute | solution.py:506
  41.4 48.4 %collective-permute-start.5 = (bf16[1,256,384]{2,1,0:T(8,128)(2,1)S(1)}, bf16[1,256,384]{2,1,0:T(8,128)(2,1)}, u32[]{:S(2)}, u32[]{:S(2)}) collective-permute-start(bf16[1,256,384]{2,1,0:T(8,128)(2,1)S(1)} %copy-done.8), channel_id=1, source_target_pairs={{0,1},{1,0},{2,3},{3,2},{4,5},{5,4},{6,7},{7,6},{8,9},{9,8},{10,11... | collective-permute-start | bytes 589832 | tf_op jit(solution)/shard_map/ppermute | solution.py:506
  43.3 46.6 %collective-permute-start.7 = (bf16[1,256,512]{2,1,0:T(8,128)(2,1)}, bf16[1,256,512]{2,1,0:T(8,128)(2,1)}, u32[]{:S(2)}, u32[]{:S(2)}) collective-permute-start(bf16[1,256,512]{2,1,0:T(8,128)(2,1)} %get-tuple-element.78.wu), channel_id=1, source_target_pairs={{0,1},{1,0},{2,3},{3,2},{4,5},{5,4},{6,7},{7,6},{8,9},{9,8},{10,11... | collective-permute-start | bytes 786440 | tf_op jit(solution)/shard_map/ppermute | solution.py:506
  233.5 4.3 %collective-permute-start.9 = (bf16[8,16,1792]{2,1,0:T(8,128)(2,1)S(1)}, bf16[8,16,1792]{2,1,0:T(8,128)(2,1)S(1)}, u32[]{:S(2)}, u32[]{:S(2)}) collective-permute-start(bf16[8,16,1792]{2,1,0:T(8,128)(2,1)S(1)} %fusion.7), channel_id=1, source_target_pairs={{0,2},{2,0},{4,6},{6,4},{8,10},{10,8},{12,14},{14,12},{16,18},{18,... | collective-permute-start | bytes 1376264 | tf_op jit(solution)/shard_map/ppermute | solution.py:506
  236.3 8.5 %collective-permute-start.14 = (bf16[4,16,1792]{2,1,0:T(8,128)(2,1)S(1)}, bf16[4,16,1792]{2,1,0:T(8,128)(2,1)S(1)}, u32[]{:S(2)}, u32[]{:S(2)}) collective-permute-start(bf16[4,16,1792]{2,1,0:T(8,128)(2,1)S(1)} %dynamic-slice_bitcast_fusion), channel_id=1, source_target_pairs={{0,4},{2,6},{4,0},{6,2},{8,12},{10,14},{12,8},{14,10},{16,20},{18,... | collective-permute-start | bytes 688136 | tf_op jit(solution)/shard_map/ppermute | solution.py:506
  238.1 10.8 %collective-permute-start.10 = (bf16[4,16,1792]{2,1,0:T(8,128)(2,1)S(1)}, bf16[4,16,1792]{2,1,0:T(8,128)(2,1)S(1)}, u32[]{:S(2)}, u32[]{:S(2)}) collective-permute-start(bf16[4,16,1792]{2,1,0:T(8,128)(2,1)S(1)} %dynamic-slice_bitcast_fusion.1), channel_id=1, source_target_pairs={{0,4},{2,6},{4,0},{6,2},{8,12},{10,14},{12,8},{14,10},{16,20},{18,... | collective-permute-start | bytes 688136 | tf_op jit(solution)/shard_map/ppermute | solution.py:506
  244.9 5.7 %collective-permute-start.15 = (bf16[2,16,1792]{2,1,0:T(8,128)(2,1)S(1)}, bf16[2,16,1792]{2,1,0:T(8,128)(2,1)S(1)}, u32[]{:S(2)}, u32[]{:S(2)}) collective-permute-start(bf16[2,16,1792]{2,1,0:T(8,128)(2,1)S(1)} %dynamic-slice_bitcast_fusion.2), channel_id=1, source_target_pairs={{0,8},{2,10},{4,12},{6,14},{8,0},{10,2},{12,4},{14,6},{16,24},{18,... | collective-permute-start | bytes 344072 | tf_op jit(solution)/shard_map/ppermute | solution.py:506
  249.0 5.5 %collective-permute-start.11 = (bf16[2,16,1792]{2,1,0:T(8,128)(2,1)S(1)}, bf16[2,16,1792]{2,1,0:T(8,128)(2,1)S(1)}, u32[]{:S(2)}, u32[]{:S(2)}) collective-permute-start(bf16[2,16,1792]{2,1,0:T(8,128)(2,1)S(1)} %dynamic-slice_bitcast_fusion.3), channel_id=1, source_target_pairs={{0,8},{2,10},{4,12},{6,14},{8,0},{10,2},{12,4},{14,6},{16,24},{18,... | collective-permute-start | bytes 344072 | tf_op jit(solution)/shard_map/ppermute | solution.py:506
  250.7 6.0 %collective-permute-start.16 = (bf16[1,16,1792]{2,1,0:T(8,128)(2,1)S(1)}, bf16[1,16,1792]{2,1,0:T(8,128)(2,1)S(1)}, u32[]{:S(2)}, u32[]{:S(2)}) collective-permute-start(bf16[1,16,1792]{2,1,0:T(8,128)(2,1)S(1)} %constant_dynamic-slice_fusion.6), channel_id=1, source_target_pairs={{0,16},{2,18},{4,20},{6,22},{8,24},{10,26},{12,28},{14,30},{16,0},... | collective-permute-start | bytes 172040 | tf_op jit(solution)/shard_map/ppermute | solution.py:506
  254.5 5.1 %collective-permute-start.12 = (bf16[1,16,1792]{2,1,0:T(8,128)(2,1)S(1)}, bf16[1,16,1792]{2,1,0:T(8,128)(2,1)S(1)}, u32[]{:S(2)}, u32[]{:S(2)}) collective-permute-start(bf16[1,16,1792]{2,1,0:T(8,128)(2,1)S(1)} %constant_dynamic-slice_fusion.7), channel_id=1, source_target_pairs={{0,16},{2,18},{4,20},{6,22},{8,24},{10,26},{12,28},{14,30},{16,0},... | collective-permute-start | bytes 172040 | tf_op jit(solution)/shard_map/ppermute | solution.py:506
  259.8 9.2 %collective-permute-start.21 = (bf16[1,16,1536]{2,1,0:T(8,128)(2,1)S(1)}, bf16[1,16,1536]{2,1,0:T(8,128)(2,1)S(1)}, u32[]{:S(2)}, u32[]{:S(2)}) collective-permute-start(bf16[1,16,1536]{2,1,0:T(8,128)(2,1)S(1)} %get-tuple-element.72), channel_id=1, source_target_pairs={{0,16},{2,18},{4,20},{6,22},{8,24},{10,26},{12,28},{14,30},{16,0},... | collective-permute-start | bytes 147464 | tf_op jit(solution)/shard_map/ppermute | solution.py:506
  262.1 8.6 %collective-permute-start.17 = (bf16[1,16,1536]{2,1,0:T(8,128)(2,1)S(1)}, bf16[1,16,1536]{2,1,0:T(8,128)(2,1)S(1)}, u32[]{:S(2)}, u32[]{:S(2)}) collective-permute-start(bf16[1,16,1536]{2,1,0:T(8,128)(2,1)S(1)} %get-tuple-element.70), channel_id=1, source_target_pairs={{0,16},{2,18},{4,20},{6,22},{8,24},{10,26},{12,28},{14,30},{16,0},... | collective-permute-start | bytes 147464 | tf_op jit(solution)/shard_map/ppermute | solution.py:506
  269.1 4.7 %collective-permute-start.22 = (bf16[2,16,1536]{2,1,0:T(8,128)(2,1)S(1)}, bf16[2,16,1536]{2,1,0:T(8,128)(2,1)S(1)}, u32[]{:S(2)}, u32[]{:S(2)}) collective-permute-start(bf16[2,16,1536]{2,1,0:T(8,128)(2,1)S(1)} %maximum_bitcast_fusion.1), channel_id=1, source_target_pairs={{0,8},{2,10},{4,12},{6,14},{8,0},{10,2},{12,4},{14,6},{16,24},{18,... | collective-permute-start | bytes 294920 | tf_op jit(solution)/shard_map/ppermute | solution.py:506
  270.7 4.7 %collective-permute-start.18 = (bf16[2,16,1536]{2,1,0:T(8,128)(2,1)S(1)}, bf16[2,16,1536]{2,1,0:T(8,128)(2,1)S(1)}, u32[]{:S(2)}, u32[]{:S(2)}) collective-permute-start(bf16[2,16,1536]{2,1,0:T(8,128)(2,1)S(1)} %maximum_bitcast_fusion), channel_id=1, source_target_pairs={{0,8},{2,10},{4,12},{6,14},{8,0},{10,2},{12,4},{14,6},{16,24},{18,... | collective-permute-start | bytes 294920 | tf_op jit(solution)/shard_map/ppermute | solution.py:506
  273.8 5.7 %collective-permute-start.23 = (bf16[4,16,1536]{2,1,0:T(8,128)(2,1)S(1)}, bf16[4,16,1536]{2,1,0:T(8,128)(2,1)S(1)}, u32[]{:S(2)}, u32[]{:S(2)}) collective-permute-start(bf16[4,16,1536]{2,1,0:T(8,128)(2,1)S(1)} %bitcast.312), channel_id=1, source_target_pairs={{0,4},{2,6},{4,0},{6,2},{8,12},{10,14},{12,8},{14,10},{16,20},{18,... | collective-permute-start | bytes 589832 | tf_op jit(solution)/shard_map/ppermute | solution.py:506
  275.4 6.2 %collective-permute-start.19 = (bf16[4,16,1536]{2,1,0:T(8,128)(2,1)S(1)}, bf16[4,16,1536]{2,1,0:T(8,128)(2,1)S(1)}, u32[]{:S(2)}, u32[]{:S(2)}) collective-permute-start(bf16[4,16,1536]{2,1,0:T(8,128)(2,1)S(1)} %bitcast.313), channel_id=1, source_target_pairs={{0,4},{2,6},{4,0},{6,2},{8,12},{10,14},{12,8},{14,10},{16,20},{18,... | collective-permute-start | bytes 589832 | tf_op jit(solution)/shard_map/ppermute | solution.py:506
  279.7 2.2 collective-permute-start.24
  281.8 12.8 %collective-permute-start.20 = (bf16[8,16,1536]{2,1,0:T(8,128)(2,1)S(1)}, bf16[8,16,1536]{2,1,0:T(8,128)(2,1)S(1)}, u32[]{:S(2)}, u32[]{:S(2)}) collective-permute-start(bf16[8,16,1536]{2,1,0:T(8,128)(2,1)S(1)} %bitcast.301), channel_id=1, source_target_pairs={{0,2},{2,0},{4,6},{6,4},{8,10},{10,8},{12,14},{14,12},{16,18},{18,... | collective-permute-start | bytes 1179656 | tf_op jit(solution)/shard_map/ppermute | solution.py:506
  (28 other events, 239.5 us)
